TPU v7x, 32 devices: a whole 2x2x4 slice. The times are simulated.
32 devices in a mesh: group: 2 (over x), chan: 16 (over z, y, core).
Axes of the slice: x: 2, y: 2, z: 4, core: 2. Of those that a mesh axis runs over, the one named last changes fastest.
Arguments:
- voltages: bfloat16 [32, 2, 256, 1024], P(('group', 'chan')), parts along dimension 0, may hold values from -6 to 6
- cal_num: float32 [32, 4, 512], P(('group', 'chan')), parts along dimension 0, may hold values from -6 to 6
- cal_weight: float32 [32, 2, 512], P(('group', 'chan')), parts along dimension 0, may hold values from 0.2 to 5
- flags: int32 [32, 512], P(('group', 'chan')), parts along dimension 0, may hold values 0 or 1
- positions: float32 [2, 512], replicated, may hold values from -300 to 300
- directions: float32 [2, 1024], replicated, may hold values from -0.05 to 0.05
- pointing: int32 [2048], P('group'), parts along dimension 0, may hold values from 0 to 1023, each once
Outputs:
- beam_power: bfloat16 [2048, 16, 128], P(('group', 'chan')), parts along dimension 0
- solved_gains: float32 [32, 4, 512], P(('group', 'chan')), parts along dimension 0
There are 2 independent parts, one for each index of `group`. A program takes and returns all parts, laid end to end along the dimension named above; an argument that names none is the same for every part. Nothing has to cross between parts.
Inputs may be any that keep to these rules, and one draw needn't show every extreme that they name: `pointing`: each table direction is named by exactly one beam.
All inputs are finite; a program needn't handle non-finite values. No bound on the sum of `flags` on one device may be relied on, other than what follows from the above.
Results may differ from a plain program's by a relative error of at most 0.004.
Values may be sent and summed in bfloat16 or wider, within the bound.
A program may use at most 64 MiB of HBM per device.

v0:
```python
import functools
import jax
import jax.numpy as jnp
from jax import lax
from jax.experimental import pallas as pl
from jax.experimental.pallas import tpu as pltpu
from jax.sharding import PartitionSpec as P

ITERS = 8
PENALTY = 2.0
RIDGE = 1.0
ORDER = 4
LANES = 128
ROUNDING = 1.5 * 2.0**23
SINE = (4.44288292, -7.30824569, 3.60635422, -0.84611165, 0.10982452)
COSINE = (1.4142135, -6.97885095, 5.73946038, -1.88355791, 0.31068803)


def basis_at(place):
    return (
        1.0,
        place,
        0.5 * (3.0 * place * place - 1.0),
        0.5 * (5.0 * place * place * place - 3.0 * place),
    )


def invert_small(matrix):
    order = len(matrix)
    unit = jnp.ones_like(matrix[0][0])
    nothing = jnp.zeros_like(unit)
    left = [list(line) for line in matrix]
    right = [[unit if row == col else nothing for col in range(order)] for row in range(order)]
    for pivot in range(order):
        factor = 1.0 / left[pivot][pivot]
        left[pivot] = [entry * factor for entry in left[pivot]]
        right[pivot] = [entry * factor for entry in right[pivot]]
        for row in range(order):
            if row != pivot:
                scale = left[row][pivot]
                left[row] = [a - scale * b for a, b in zip(left[row], left[pivot])]
                right[row] = [a - scale * b for a, b in zip(right[row], right[pivot])]
    return right


def horner(coefficients, value):
    total = coefficients[-1] * value + coefficients[-2]
    for entry in coefficients[-3::-1]:
        total = total * value + entry
    return total


def tile_at(step, mine, tiles):
    if tiles == 4:
        high = lax.rem(mine // 2 + 1 - step // 2, 2)
        low = lax.rem(lax.rem(mine, 2) + (step + 1) // 2, 2)
        return 2 * high + low
    return lax.rem(mine + tiles // 2 + step, tiles)


def combine(factors, terms):
    total = terms[0] * factors[0]
    for factor, term in zip(factors[1:], terms[1:]):
        total = total + factor * term
    return total


def tree(terms):
    while len(terms) > 1:
        terms = [sum(terms[at : at + 2]) if at + 1 < len(terms) else terms[at] for at in range(0, len(terms), 2)]
    return terms[0]


def kernel(
    n,
    tiles,
    volts_hbm,
    num_hbm,
    weight_hbm,
    flags_hbm,
    positions_hbm,
    directions_hbm,
    pointing_hbm,
    power_ref,
    gains_ref,
    num_ref,
    weight_ref,
    flags_ref,
    positions_ref,
    directions_ref,
    pointing_ref,
    volts,
    message,
    gathered,
    outbox,
    inbox,
    ordered,
    products,
    phasors,
    ready,
    columns,
    table,
    pointed,
    local_ref,
    dual_ref,
    load_sem,
    cal_send,
    cal_recv,
    fit_send,
    fit_recv,
    out_send,
    out_recv,
    own_sem,
):
    me = lax.axis_index("chan")
    stations = flags_ref.shape[1]
    blocks = stations // LANES
    width = phasors.shape[2]
    samples = volts.shape[1]
    half = samples // 2
    per_device = ready.shape[0] // n
    per_tile = n // tiles
    share = lax.rem(me, blocks)

    loads = [
        pltpu.make_async_copy(source, target, load_sem.at[index])
        for index, (source, target) in enumerate(
            (
                (num_hbm.at[0], num_ref),
                (weight_hbm.at[0], weight_ref),
                (flags_hbm, flags_ref),
                (positions_hbm, positions_ref),
                (directions_hbm, directions_ref),
                (pointing_hbm, pointing_ref),
                (volts_hbm.at[0], volts),
            )
        )
    ]
    for load in loads:
        load.start()

    barrier = pltpu.get_barrier_semaphore()

    @pl.loop(1, n)
    def _(offset):
        pl.semaphore_signal(
            barrier,
            inc=1,
            device_id={"chan": lax.rem(me + offset, n)},
            device_id_type=pl.DeviceIdType.MESH,
        )

    for load in loads[:3]:
        load.wait()
    for block in range(blocks):
        lanes = pl.ds(block * LANES, LANES)
        mask = flags_ref[:, lanes].astype(jnp.float32)
        message[block, 0:4, :] = mask * num_ref[:, lanes]
        for row in range(4):
            message[block, pl.ds(4 + row, 1), :] = mask * weight_ref[pl.ds(row // 2, 1), lanes]
    gathered[me] = message[share]

    pl.semaphore_wait(barrier, n - 1)

    def cal_copy(block, slot, peer, sent, received):
        return pltpu.make_async_remote_copy(
            src_ref=message.at[block],
            dst_ref=gathered.at[slot],
            send_sem=cal_send.at[sent],
            recv_sem=cal_recv.at[received],
            device_id={"chan": peer},
            device_id_type=pl.DeviceIdType.MESH,
        )

    @pl.loop(1, n)
    def _(offset):
        peer = lax.rem(me + offset, n)
        cal_copy(lax.rem(peer, blocks), me, peer, peer, me).start()

    for load in loads[3:6]:
        load.wait()
    for axis in range(2):
        for block in range(blocks):
            lanes = pl.ds(block * LANES, LANES)
            row = jnp.broadcast_to(positions_ref[pl.ds(axis, 1), lanes], (LANES, LANES))
            columns[axis, lanes, :] = row.T

    rest = directions_ref[...]
    table[...] = jnp.zeros_like(table)
    for term in range(3):
        head = rest.astype(jnp.bfloat16).astype(jnp.float32)
        table[pl.ds(8 * term, 2), :] = head
        rest = rest - head
    ratio = 1.0 + 0.15 * (2.0 * (me.astype(jnp.float32) + 0.5) / n)
    entries = directions_ref.shape[1]
    chunk = 32

    @pl.loop(0, tiles)
    def _(tile):
        numbers = lax.broadcasted_iota(jnp.int32, (entries, width), 0)
        chosen = jnp.where(numbers == pointing_ref[tile], 1.0, 0.0).astype(jnp.bfloat16)
        terms = table[...].astype(jnp.bfloat16)
        found = jnp.dot(terms, chosen, preferred_element_type=jnp.float32)
        pointed[tile] = (found[0:8] + found[8:16] + found[16:24]) * ratio

    def make_phasors(step):
        tile = tile_at(step, me // per_tile, tiles)
        east = pointed[tile, 0:1, :]
        north = pointed[tile, 1:2, :]

        @pl.loop(0, stations // chunk)
        def _(part):
            rows = pl.ds(pl.multiple_of(part * chunk, chunk), chunk)
            below = pl.ds(pl.multiple_of(stations + part * chunk, chunk), chunk)
            for piece in range(width // LANES):
                lanes = pl.ds(piece * LANES, LANES)
                cut = slice(piece * LANES, (piece + 1) * LANES)
                turns = columns[0, rows, :] * east[:, cut] + columns[1, rows, :] * north[:, cut]
                turns = turns - ((turns + ROUNDING) - ROUNDING)
                square = turns * turns
                sine = horner(SINE, square) * turns
                cosine = horner(COSINE, square)
                phasors[step, rows, lanes] = (1.0 - sine * sine).astype(jnp.bfloat16)
                phasors[step, below, lanes] = (sine * cosine).astype(jnp.bfloat16)

    make_phasors(0)

    @pl.loop(1, n)
    def _(offset):
        peer = lax.rem(me + offset, n)
        cal_copy(0, peer, peer, peer, peer).wait_recv()

    pairs = n // 2
    basis = [basis_at(2.0 * (n - pair - 0.5) / n - 1.0) for pair in range(pairs)]
    sign = jnp.where(lax.broadcasted_iota(jnp.int32, (8, LANES), 0) < 4, 1.0, -1.0)
    solve_rows = []
    for pair in range(pairs):
        first = gathered[n - 1 - pair]
        second = gathered[pair]
        weight = jnp.concatenate([first[4:8], second[4:8]], axis=0)
        usable = jnp.where(weight > 0.0, 1.0, 0.0)
        damping = 1.0 / (weight + PENALTY)
        target = jnp.concatenate([first[0:4], second[0:4]], axis=0) * damping
        solve_rows.append((usable, PENALTY * damping, target))

    def both(term, value):
        value = value * sign if term % 2 else value
        return value + pltpu.roll(value, 4, 0)

    gram = [[None] * ORDER for _ in range(ORDER)]
    for first in range(ORDER):
        for second in range(first, ORDER):
            terms = [
                (basis[pair][first] * basis[pair][second]) * solve_rows[pair][0]
                for pair in range(pairs)
            ]
            gram[first][second] = both(first + second, tree(terms))
            gram[second][first] = gram[first][second]
        gram[first][first] = gram[first][first] + RIDGE
    inverse = invert_small(gram)
    local_ref[...] = jnp.zeros_like(local_ref)
    dual_ref[...] = jnp.zeros_like(dual_ref)
    nothing = jnp.zeros((8, LANES), jnp.float32)

    def sweep(_, line):
        signed = [entry * sign if term % 2 else entry for term, entry in enumerate(line)]
        numerator = [[] for _ in range(ORDER)]
        for pair in range(pairs):
            values = basis[pair]
            usable, damping, target = solve_rows[pair]
            fitted = tree([signed[0]] + [values[term] * signed[term] for term in range(1, ORDER)])
            dual = dual_ref[pair] + usable * (local_ref[pair] - fitted)
            local = target + damping * (fitted - dual)
            local_ref[pair] = local
            dual_ref[pair] = dual
            summand = usable * (local + dual)
            for term in range(ORDER):
                numerator[term].append(values[term] * summand if term else summand)
        sums = [both(term, tree(terms)) for term, terms in enumerate(numerator)]
        return tuple(
            tree([entry * total for entry, total in zip(inverse[first], sums)])
            for first in range(ORDER)
        )

    line = lax.fori_loop(0, ITERS, sweep, (nothing,) * ORDER)
    line = [entry[0:4] for entry in line]

    def fitted_at(channel):
        return combine(basis_at(2.0 * (channel.astype(jnp.float32) + 0.5) / n - 1.0), line)

    def fit_copy(source, slot, peer, sent, received):
        return pltpu.make_async_remote_copy(
            src_ref=outbox.at[source],
            dst_ref=inbox.at[slot],
            send_sem=fit_send.at[sent],
            recv_sem=fit_recv.at[received],
            device_id={"chan": peer},
            device_id_type=pl.DeviceIdType.MESH,
        )

    for offset in range(1, blocks):
        mate = lax.rem(share + offset, blocks)
        peer = me - share + mate
        outbox[mate] = fitted_at(peer)
        fit_copy(mate, share, peer, mate, share).start()
    inbox[share] = fitted_at(me)

    loads[6].wait()
    row = lax.broadcasted_iota(jnp.int32, (samples, samples), 0)
    col = lax.broadcasted_iota(jnp.int32, (samples, samples), 1)
    origin = jnp.where(row < half, 2 * row, 2 * (row - half) + 1)
    shuffle = jnp.where(col == origin, 1.0, 0.0).astype(jnp.bfloat16)
    for polar in range(2):
        ordered[polar] = jnp.dot(shuffle, volts[polar], preferred_element_type=jnp.float32)

    make_phasors(1)
    for offset in range(1, blocks):
        mate = lax.rem(share + offset, blocks)
        fit_copy(mate, mate, me - share + mate, mate, mate).wait_recv()
    for block in range(blocks):
        gains_ref[0, :, pl.ds(block * LANES, LANES)] = inbox[block]

    scale = flags_ref[...].astype(jnp.float32) * stations ** (-0.5)
    strip = 64
    for polar in range(2):
        gain_re = gains_ref[0, pl.ds(2 * polar, 1), :] * scale
        gain_im = gains_ref[0, pl.ds(2 * polar + 1, 1), :] * scale

        @pl.loop(0, samples // strip)
        def _(step):
            rows = pl.ds(pl.multiple_of(step * strip, strip), strip)
            real = ordered[polar, rows, :stations]
            imag = ordered[polar, rows, stations:]
            new_re = (gain_re * real + gain_im * imag).astype(jnp.bfloat16)
            new_im = (gain_re * imag - gain_im * real).astype(jnp.bfloat16)
            upper = pl.ds(pl.multiple_of(2 * polar * samples + step * strip, strip), strip)
            lower = pl.ds(pl.multiple_of((2 * polar + 1) * samples + step * strip, strip), strip)
            products[upper, :stations] = new_re
            products[upper, stations:] = new_im
            products[lower, :stations] = new_im
            products[lower, stations:] = -new_re

    def out_copy(owner, source, sent, received):
        rows = pl.ds(pl.multiple_of(owner * per_device, per_device), per_device)
        return pltpu.make_async_remote_copy(
            src_ref=ready.at[rows, :],
            dst_ref=power_ref.at[source],
            send_sem=out_send.at[sent],
            recv_sem=out_recv.at[received],
            device_id={"chan": owner},
            device_id_type=pl.DeviceIdType.MESH,
        )

    def own_copy():
        rows = pl.ds(pl.multiple_of(me * per_device, per_device), per_device)
        return pltpu.make_async_copy(ready.at[rows, :], power_ref.at[me], own_sem)

    @pl.loop(0, tiles)
    def _(step):
        @pl.when(step >= 2)
        def _():
            make_phasors(step)

        tile = tile_at(step, me // per_tile, tiles)
        beams = jnp.dot(products[...], phasors[step], preferred_element_type=jnp.float32)
        total = beams[:samples] * beams[:samples]
        for part in range(1, 4):
            piece = beams[part * samples : (part + 1) * samples]
            total = total + piece * piece
        mean = (total[:half] + total[half:]) * 0.5
        rows = pl.ds(pl.multiple_of(tile * width, width), width)
        ready[rows, :] = mean.T.astype(jnp.bfloat16)

        @pl.loop(0, per_tile)
        def _(index):
            owner = tile * per_tile + index

            @pl.when(owner != me)
            def _():
                out_copy(owner, me, owner, me).start()

            @pl.when(owner == me)
            def _():
                own_copy().start()

    own_copy().wait()
    for offset in range(1, blocks):
        mate = lax.rem(share + offset, blocks)
        fit_copy(mate, share, me - share + mate, mate, share).wait_send()

    @pl.loop(1, n)
    def _(offset):
        peer = lax.rem(me + offset, n)
        cal_copy(lax.rem(peer, blocks), me, peer, peer, me).wait_send()
        out_copy(peer, me, peer, me).wait_send()
        out_copy(peer, peer, peer, peer).wait_recv()


def body(voltages, cal_num, cal_weight, flags, positions, directions, pointing):
    n = lax.axis_size("chan")
    count, polars, samples, depth = voltages.shape
    stations = flags.shape[1]
    blocks = stations // LANES
    assert count == 1 and polars == 2 and n % blocks == 0 and n % 2 == 0
    beams = pointing.shape[0]
    tiles = 4
    width = beams // tiles
    half = samples // 2
    entries = directions.shape[1]
    vmem = pl.BlockSpec(memory_space=pltpu.VMEM)
    hbm = pl.BlockSpec(memory_space=pltpu.HBM)
    f32 = jnp.float32
    power, gains = pl.pallas_call(
        functools.partial(kernel, n, tiles),
        out_shape=(
            pltpu.VMEM((n, beams // n, half), jnp.bfloat16),
            jax.ShapeDtypeStruct(cal_num.shape, f32),
        ),
        in_specs=[hbm] * 7,
        out_specs=(vmem, vmem),
        scratch_shapes=[
            pltpu.VMEM(cal_num.shape[1:], f32),
            pltpu.VMEM(cal_weight.shape[1:], f32),
            pltpu.VMEM(flags.shape, jnp.int32),
            pltpu.VMEM(positions.shape, f32),
            pltpu.VMEM(directions.shape, f32),
            pltpu.VMEM((tiles, 1, width), jnp.int32),
            pltpu.VMEM((polars, samples, depth), jnp.bfloat16),
            pltpu.VMEM((blocks, 8, LANES), f32),
            pltpu.VMEM((n, 8, LANES), f32),
            pltpu.VMEM((blocks, 4, LANES), f32),
            pltpu.VMEM((blocks, 4, LANES), f32),
            pltpu.VMEM((polars, samples, depth), f32),
            pltpu.VMEM((4 * samples, depth), jnp.bfloat16),
            pltpu.VMEM((tiles, depth, width), jnp.bfloat16),
            pltpu.VMEM((beams, half), jnp.bfloat16),
            pltpu.VMEM((2, stations, LANES), f32),
            pltpu.VMEM((32, entries), f32),
            pltpu.VMEM((tiles, 8, width), f32),
            pltpu.VMEM((n // 2, 8, LANES), f32),
            pltpu.VMEM((n // 2, 8, LANES), f32),
            pltpu.SemaphoreType.DMA((7,)),
            pltpu.SemaphoreType.DMA((n,)),
            pltpu.SemaphoreType.DMA((n,)),
            pltpu.SemaphoreType.DMA((blocks,)),
            pltpu.SemaphoreType.DMA((blocks,)),
            pltpu.SemaphoreType.DMA((n,)),
            pltpu.SemaphoreType.DMA((n,)),
            pltpu.SemaphoreType.DMA,
        ],
        compiler_params=pltpu.CompilerParams(
            collective_id=0, has_side_effects=True, vmem_limit_bytes=40 * 2**20
        ),
    )(
        *(
            pltpu.with_memory_space_constraint(operand, pltpu.HBM)
            for operand in (
                voltages,
                cal_num,
                cal_weight,
                flags,
                positions,
                directions,
                pointing.reshape(tiles, 1, width),
            )
        )
    )
    return jnp.transpose(power, (1, 0, 2)), gains


def solution(mesh):
    return jax.shard_map(
        body,
        mesh=mesh,
        in_specs=(
            P(("group", "chan"), None, None, None),
            P(("group", "chan"), None, None),
            P(("group", "chan"), None, None),
            P(("group", "chan"), None),
            P(),
            P(),
            P("group"),
        ),
        out_specs=(P(("group", "chan"), None, None), P(("group", "chan"), None, None)),
        check_vma=False,
    )
```

profile of v0, /device:TPU:0, one launch (start us, length us, event | category | flops | bytes accessed | tf_op | source)
XLA Modules:
  0.0 23.0 jit_solution(160664383069355)
XLA Ops:
  0.6 20.9 %shard_map.86 = (bf16[16,64,128]{2,1,0:T(8,128)(2,1)S(1)}, f32[1,4,512]{2,1,0:T(4,128)S(1)}) custom-call(bf16[1,2,256,1024]{3,2,1,0:T(8,128)(2,1)} %volts_hbm.1, f32[1,4,512]{2,1,0:T(4,128)} %num_hbm.1, f32[1,2,512]{2,1,0:T(2,128)} %weight_hbm.1, s32[1,512]{1,0:T(1,128)} %flags_hbm.1, f32[2,512]{1,0:T(2,128)} %positions_hbm.1, f32[2,1024]{1,0:T(2,128)} %directions_hbm.1, ...), custom_call_target="tpu_custom_call" | custom-call | tf_op jit(solution)/shard_map/pallas_call | solution.py:413
  21.5 0.9 %copy.9 = bf16[64,16,128]{2,1,0:T(8,128)(2,1)} copy(bf16[64,16,128]{2,0,1:T(8,128)(2,1)S(1)} %bitcast.2) | data formatting | bytes 524288
  22.4 0.6 %copy.11 = f32[1,4,512]{2,1,0:T(4,128)} copy(f32[1,4,512]{2,1,0:T(4,128)S(1)} %get-tuple-element.11) | data formatting | bytes 16384
where the time goes:
time: 23.2 us; the launch traced here: 23 us
  Pallas kernels  20.9 us (90%)
  local copies, waits for them, and re-layouts  1.47 us (6%)
  between operations  0.64 us (3%)
    pallas_call x1, Pallas kernels, body(): pl.pallas_call(functools.partial(kernel, n, tiles), out_shape=(pltpu.VMEM...  20.9 us
    unnamed x2, local copies, waits for them, and re-layouts  1.47 us

commit v1 on v0

--- a/solution.py
+++ b/solution.py
@@ -12,7 +12,7 @@
 ORDER = 4
 LANES = 128
 ROUNDING = 1.5 * 2.0**23
-SINE = (4.44288292, -7.30824569, 3.60635422, -0.84611165, 0.10982452)
+SINE = (4.44287957, -7.30781668, 3.59777418, -0.79119939)
 COSINE = (1.4142135, -6.97885095, 5.73946038, -1.88355791, 0.31068803)
 
 
@@ -141,12 +141,15 @@
 
     barrier = pltpu.get_barrier_semaphore()
 
+    def far_first(offset):
+        return 1 + lax.rem(offset + n // 2 - 2, n - 1)
+
     @pl.loop(1, n)
     def _(offset):
         pl.semaphore_signal(
             barrier,
             inc=1,
-            device_id={"chan": lax.rem(me + offset, n)},
+            device_id={"chan": lax.rem(me + far_first(offset), n)},
             device_id_type=pl.DeviceIdType.MESH,
         )
 
@@ -174,7 +177,7 @@
 
     @pl.loop(1, n)
     def _(offset):
-        peer = lax.rem(me + offset, n)
+        peer = lax.rem(me + far_first(offset), n)
         cal_copy(lax.rem(peer, blocks), me, peer, peer, me).start()
 
     for load in loads[3:6]:
@@ -393,6 +396,10 @@
         peer = lax.rem(me + offset, n)
         cal_copy(lax.rem(peer, blocks), me, peer, peer, me).wait_send()
         out_copy(peer, me, peer, me).wait_send()
+
+    @pl.loop(1, n)
+    def _(offset):
+        peer = lax.rem(me + offset, n)
         out_copy(peer, peer, peer, peer).wait_recv()
 
 

time: 23.2 us -> 23.4 us (level)
  no operation moved by 1% of the time
where the time goes in v1:
time: 23.4 us; the launch traced here: 23.2 us
  Pallas kernels  21.1 us (90%)
  local copies, waits for them, and re-layouts  1.47 us (6%)
  between operations  0.64 us (3%)
    pallas_call x1, Pallas kernels, body(): pl.pallas_call(functools.partial(kernel, n, tiles), out_shape=(pltpu.VMEM...  21.1 us
    unnamed x2, local copies, waits for them, and re-layouts  1.47 us

profile of v1, /device:TPU:0, one launch (start us, length us, event | category | flops | bytes accessed | tf_op | source)
XLA Modules:
  0.0 23.2 jit_solution(1578689133171040647)
XLA Ops:
  0.6 21.1 %shard_map.86 = (bf16[16,64,128]{2,1,0:T(8,128)(2,1)S(1)}, f32[1,4,512]{2,1,0:T(4,128)S(1)}) custom-call(bf16[1,2,256,1024]{3,2,1,0:T(8,128)(2,1)} %volts_hbm.1, f32[1,4,512]{2,1,0:T(4,128)} %num_hbm.1, f32[1,2,512]{2,1,0:T(2,128)} %weight_hbm.1, s32[1,512]{1,0:T(1,128)} %flags_hbm.1, f32[2,512]{1,0:T(2,128)} %positions_hbm.1, f32[2,1024]{1,0:T(2,128)} %directions_hbm.1, ...), custom_call_target="tpu_custom_call" | custom-call | tf_op jit(solution)/shard_map/pallas_call | solution.py:420
  21.7 0.9 %copy.9 = bf16[64,16,128]{2,1,0:T(8,128)(2,1)} copy(bf16[64,16,128]{2,0,1:T(8,128)(2,1)S(1)} %bitcast.2) | data formatting | bytes 524288
  22.6 0.6 %copy.11 = f32[1,4,512]{2,1,0:T(4,128)} copy(f32[1,4,512]{2,1,0:T(4,128)S(1)} %get-tuple-element.11) | data formatting | bytes 16384

commit v2 on v0

--- a/solution.py
+++ b/solution.py
@@ -115,7 +115,7 @@
     me = lax.axis_index("chan")
     stations = flags_ref.shape[1]
     blocks = stations // LANES
-    width = phasors.shape[2]
+    width = phasors.shape[2] // 2
     samples = volts.shape[1]
     half = samples // 2
     per_device = ready.shape[0] // n
@@ -204,6 +204,7 @@
         pointed[tile] = (found[0:8] + found[8:16] + found[16:24]) * ratio
 
     def make_phasors(step):
+        group, side = step // 2, step % 2
         tile = tile_at(step, me // per_tile, tiles)
         east = pointed[tile, 0:1, :]
         north = pointed[tile, 1:2, :]
@@ -213,15 +214,15 @@
             rows = pl.ds(pl.multiple_of(part * chunk, chunk), chunk)
             below = pl.ds(pl.multiple_of(stations + part * chunk, chunk), chunk)
             for piece in range(width // LANES):
-                lanes = pl.ds(piece * LANES, LANES)
+                lanes = pl.ds(side * width + piece * LANES, LANES)
                 cut = slice(piece * LANES, (piece + 1) * LANES)
                 turns = columns[0, rows, :] * east[:, cut] + columns[1, rows, :] * north[:, cut]
                 turns = turns - ((turns + ROUNDING) - ROUNDING)
                 square = turns * turns
                 sine = horner(SINE, square) * turns
                 cosine = horner(COSINE, square)
-                phasors[step, rows, lanes] = (1.0 - sine * sine).astype(jnp.bfloat16)
-                phasors[step, below, lanes] = (sine * cosine).astype(jnp.bfloat16)
+                phasors[group, rows, lanes] = (1.0 - sine * sine).astype(jnp.bfloat16)
+                phasors[group, below, lanes] = (sine * cosine).astype(jnp.bfloat16)
 
     make_phasors(0)
 
@@ -355,33 +356,36 @@
         rows = pl.ds(pl.multiple_of(me * per_device, per_device), per_device)
         return pltpu.make_async_copy(ready.at[rows, :], power_ref.at[me], own_sem)
 
-    @pl.loop(0, tiles)
-    def _(step):
-        @pl.when(step >= 2)
+    @pl.loop(0, tiles // 2)
+    def _(group):
+        @pl.when(group > 0)
         def _():
-            make_phasors(step)
-
-        tile = tile_at(step, me // per_tile, tiles)
-        beams = jnp.dot(products[...], phasors[step], preferred_element_type=jnp.float32)
+            for step in range(2, tiles):
+                make_phasors(step)
+
+        beams = jnp.dot(products[...], phasors[group], preferred_element_type=jnp.float32)
         total = beams[:samples] * beams[:samples]
         for part in range(1, 4):
             piece = beams[part * samples : (part + 1) * samples]
             total = total + piece * piece
         mean = (total[:half] + total[half:]) * 0.5
-        rows = pl.ds(pl.multiple_of(tile * width, width), width)
-        ready[rows, :] = mean.T.astype(jnp.bfloat16)
-
-        @pl.loop(0, per_tile)
-        def _(index):
-            owner = tile * per_tile + index
-
-            @pl.when(owner != me)
-            def _():
-                out_copy(owner, me, owner, me).start()
-
-            @pl.when(owner == me)
-            def _():
-                own_copy().start()
+        for side in range(2):
+            tile = tile_at(2 * group + side, me // per_tile, tiles)
+            rows = pl.ds(pl.multiple_of(tile * width, width), width)
+            own = mean[:, side * width : (side + 1) * width]
+            ready[rows, :] = own.T.astype(jnp.bfloat16)
+
+            @pl.loop(0, per_tile)
+            def _(index):
+                owner = tile * per_tile + index
+
+                @pl.when(owner != me)
+                def _():
+                    out_copy(owner, me, owner, me).start()
+
+                @pl.when(owner == me)
+                def _():
+                    own_copy().start()
 
     own_copy().wait()
     for offset in range(1, blocks):
@@ -432,7 +436,7 @@
             pltpu.VMEM((blocks, 4, LANES), f32),
             pltpu.VMEM((polars, samples, depth), f32),
             pltpu.VMEM((4 * samples, depth), jnp.bfloat16),
-            pltpu.VMEM((tiles, depth, width), jnp.bfloat16),
+            pltpu.VMEM((tiles // 2, depth, 2 * width), jnp.bfloat16),
             pltpu.VMEM((beams, half), jnp.bfloat16),
             pltpu.VMEM((2, stations, LANES), f32),
             pltpu.VMEM((32, entries), f32),

time: 23.2 us -> 24.1 us (1.039)
  the two profiles are of different devices: /device:TPU:0 before, /device:TPU:1 now
where the time goes in v2:
time: 24.1 us; the launch traced here: 23.9 us
  Pallas kernels  21.8 us (90%)
  local copies, waits for them, and re-layouts  1.47 us (6%)
  between operations  0.64 us (3%)
    pallas_call x1, Pallas kernels, body(): pl.pallas_call(functools.partial(kernel, n, tiles), out_shape=(pltpu.VMEM...  21.8 us
    unnamed x2, local copies, waits for them, and re-layouts  1.47 us

profile of v2, /device:TPU:1, one launch (start us, length us, event | category | flops | bytes accessed | tf_op | source)
XLA Modules:
  0.0 23.9 jit_solution(12695845491852859122)
XLA Ops:
  0.6 21.8 %shard_map.86 = (bf16[16,64,128]{2,1,0:T(8,128)(2,1)S(1)}, f32[1,4,512]{2,1,0:T(4,128)S(1)}) custom-call(bf16[1,2,256,1024]{3,2,1,0:T(8,128)(2,1)} %volts_hbm.1, f32[1,4,512]{2,1,0:T(4,128)} %num_hbm.1, f32[1,2,512]{2,1,0:T(2,128)} %weight_hbm.1, s32[1,512]{1,0:T(1,128)} %flags_hbm.1, f32[2,512]{1,0:T(2,128)} %positions_hbm.1, f32[2,1024]{1,0:T(2,128)} %directions_hbm.1, ...), custom_call_target="tpu_custom_call" | custom-call | tf_op jit(solution)/shard_map/pallas_call | solution.py:417
  22.4 0.9 %copy.9 = bf16[64,16,128]{2,1,0:T(8,128)(2,1)} copy(bf16[64,16,128]{2,0,1:T(8,128)(2,1)S(1)} %bitcast.2) | data formatting | bytes 524288
  23.3 0.6 %copy.11 = f32[1,4,512]{2,1,0:T(4,128)} copy(f32[1,4,512]{2,1,0:T(4,128)S(1)} %get-tuple-element.11) | data formatting | bytes 16384

commit v3 on v0

--- a/solution.py
+++ b/solution.py
@@ -313,7 +313,6 @@
     for polar in range(2):
         ordered[polar] = jnp.dot(shuffle, volts[polar], preferred_element_type=jnp.float32)
 
-    make_phasors(1)
     for offset in range(1, blocks):
         mate = lax.rem(share + offset, blocks)
         fit_copy(mate, mate, me - share + mate, mate, mate).wait_recv()
@@ -357,7 +356,7 @@
 
     @pl.loop(0, tiles)
     def _(step):
-        @pl.when(step >= 2)
+        @pl.when(step >= 1)
         def _():
             make_phasors(step)
 

time: 23.2 us -> 24 us (1.034)
  Pallas kernels: 20.9 us -> 21.7 us
    pallas_call x1, Pallas kernels: 20.9 us -> 21.7 us  [body(): pl.pallas_call(functools.partial(kernel, n, tiles), out_shape=(pltpu.VMEM...]
where the time goes in v3:
time: 24 us; the launch traced here: 23.8 us
  Pallas kernels  21.7 us (90%)
  local copies, waits for them, and re-layouts  1.47 us (6%)
  between operations  0.64 us (3%)
    pallas_call x1, Pallas kernels, body(): pl.pallas_call(functools.partial(kernel, n, tiles), out_shape=(pltpu.VMEM...  21.7 us
    unnamed x2, local copies, waits for them, and re-layouts  1.47 us

profile of v3, /device:TPU:0, one launch (start us, length us, event | category | flops | bytes accessed | tf_op | source)
XLA Modules:
  0.0 23.8 jit_solution(17238997166521166380)
XLA Ops:
  0.6 21.7 %shard_map.86 = (bf16[16,64,128]{2,1,0:T(8,128)(2,1)S(1)}, f32[1,4,512]{2,1,0:T(4,128)S(1)}) custom-call(bf16[1,2,256,1024]{3,2,1,0:T(8,128)(2,1)} %volts_hbm.1, f32[1,4,512]{2,1,0:T(4,128)} %num_hbm.1, f32[1,2,512]{2,1,0:T(2,128)} %weight_hbm.1, s32[1,512]{1,0:T(1,128)} %flags_hbm.1, f32[2,512]{1,0:T(2,128)} %positions_hbm.1, f32[2,1024]{1,0:T(2,128)} %directions_hbm.1, ...), custom_call_target="tpu_custom_call" | custom-call | tf_op jit(solution)/shard_map/pallas_call | solution.py:412
  22.3 0.9 %copy.9 = bf16[64,16,128]{2,1,0:T(8,128)(2,1)} copy(bf16[64,16,128]{2,0,1:T(8,128)(2,1)S(1)} %bitcast.2) | data formatting | bytes 524288
  23.2 0.6 %copy.11 = f32[1,4,512]{2,1,0:T(4,128)} copy(f32[1,4,512]{2,1,0:T(4,128)S(1)} %get-tuple-element.11) | data formatting | bytes 16384
